TPU v7x, 32 devices: a whole 2x2x4 slice. The times are simulated.
32 devices in a mesh: dp: 8 (over y, x, core), seq: 4 (over z).
Axes of the slice: x: 2, y: 2, z: 4, core: 2. Of those that a mesh axis runs over, the one named last changes fastest.
Arguments:
- inputs: bfloat16 [32768, 768], P(('dp', 'seq')), may hold values from -6 to 6
- attn_gain: bfloat16 [768], P('dp'), may hold values from 0.25 to 1.75
- qkv_weight: bfloat16 [768, 2304], P('dp'), may hold values from -0.25 to 0.25
- proj_weight: bfloat16 [768, 768], P('dp'), may hold values from -0.4375 to 0.4375
- mlp_gain: bfloat16 [768], P('dp'), may hold values from 0.25 to 1.75
- in_weight: bfloat16 [768, 2304], P('dp'), may hold values from -0.21875 to 0.21875
- out_weight: bfloat16 [1152, 768], P('dp'), may hold values from -0.25 to 0.25
- cotangent: bfloat16 [32768, 768], P(('dp', 'seq')), may hold values from -12 to 12
Outputs:
- output: bfloat16 [32768, 768], P(('dp', 'seq'))
- input_grad: bfloat16 [32768, 768], P(('dp', 'seq'))
- attn_gain_grad: float32 [768], P('dp')
- qkv_weight_grad: float32 [768, 2304], P('dp')
- proj_weight_grad: float32 [768, 768], P('dp')
- mlp_gain_grad: float32 [768], P('dp')
- in_weight_grad: float32 [768, 2304], P('dp')
- out_weight_grad: float32 [1152, 768], P('dp')
All inputs are finite; a program needn't handle non-finite values.
Results may differ from a plain program's by a relative error of at most 0.02.
Values may be sent and summed in bfloat16 or wider, within the bound.
A program may use at most 128 MiB of HBM per device.

v0:
```python
import jax
import jax.numpy as jnp
from jax import lax
from jax.sharding import PartitionSpec as P

D = 768
HEADS = 12
HEAD_DIM = 64
FF = 1152
WINDOW = 64
QBLOCK = 512
epsilon = 1e-05
theta_base = 10000.0
masked_score = -1e30


def layer_norm(features, gain_vector):
    center = features - jnp.mean(features, -1, keepdims=True)
    spread = jnp.mean(center * center, -1, keepdims=True)
    return center * lax.rsqrt(spread + epsilon) * gain_vector


def rotary_tables(positions, head_width):
    half_width = head_width // 2
    inverse_freq = theta_base ** (-(jnp.arange(half_width, dtype=jnp.float32) * 2.0) / head_width)
    angles = positions[:, None] * inverse_freq[None, :]
    cosine_table = jnp.concatenate([jnp.cos(angles), jnp.cos(angles)], -1)
    sine_table = jnp.concatenate([jnp.sin(angles), jnp.sin(angles)], -1)
    return (cosine_table[:, None, :], sine_table[:, None, :])


def rotate(features, cosine_table, sine_table):
    half_width = features.shape[-1] // 2
    turned = jnp.concatenate([-features[..., half_width:], features[..., :half_width]], -1)
    return features * cosine_table + turned * sine_table


def gated_gelu(up_values):
    gelu_input = up_values[:, :FF]
    gate_half = up_values[:, FF:]
    return jax.nn.gelu(gelu_input, approximate=False) * gate_half


def band_scores(query_block, key_block, first_row, seq_total):
    score_scale = query_block.shape[-1] ** (-0.5)
    key_span = key_block.shape[0]
    scores = (
        jnp.einsum("qhd,khd->hqk", query_block, key_block, preferred_element_type=jnp.float32)
        * score_scale
    )
    query_pos = first_row + jnp.arange(QBLOCK, dtype=jnp.int32)[:, None]
    key_pos = first_row - WINDOW + jnp.arange(key_span, dtype=jnp.int32)[None, :]
    in_band = (jnp.abs(query_pos - key_pos) <= WINDOW) & (key_pos >= 0) & (key_pos < seq_total)
    return jnp.where(in_band[None], scores, masked_score)


def band_forward(queries, key_pad, value_pad, offset, seq_total):
    row_count = queries.shape[0]
    key_span = QBLOCK + 2 * WINDOW

    def one_block(block_index):
        row_start = block_index * QBLOCK
        query_block = lax.dynamic_slice_in_dim(queries, row_start, QBLOCK, 0)
        key_block = lax.dynamic_slice_in_dim(key_pad, row_start, key_span, 0)
        value_block = lax.dynamic_slice_in_dim(value_pad, row_start, key_span, 0)
        scores = band_scores(query_block, key_block, offset + row_start, seq_total)
        row_max = jnp.max(scores, -1, keepdims=True)
        weights = jnp.exp(scores - row_max)
        row_sum = jnp.sum(weights, -1, keepdims=True)
        softmax_low = (weights / row_sum).astype(jnp.bfloat16)
        result = jnp.einsum(
            "hqk,khd->qhd", softmax_low, value_block, preferred_element_type=jnp.float32
        )
        log_sum = jnp.transpose((row_max + jnp.log(row_sum))[:, :, 0])
        return (result, log_sum)

    results, log_sums = lax.map(one_block, jnp.arange(row_count // QBLOCK, dtype=jnp.int32))
    return (results.reshape(queries.shape), log_sums.reshape(row_count, queries.shape[1]))


def band_backward(queries, key_pad, value_pad, grad_out, log_sums, offset, seq_total):
    row_count = queries.shape[0]
    key_span = QBLOCK + 2 * WINDOW
    score_scale = queries.shape[-1] ** (-0.5)

    def one_block(carried, block_index):
        key_grads, value_grads = carried
        row_start = block_index * QBLOCK
        query_block = lax.dynamic_slice_in_dim(queries, row_start, QBLOCK, 0)
        key_block = lax.dynamic_slice_in_dim(key_pad, row_start, key_span, 0)
        value_block = lax.dynamic_slice_in_dim(value_pad, row_start, key_span, 0)
        grad_block = lax.dynamic_slice_in_dim(grad_out, row_start, QBLOCK, 0)
        lse_block = lax.dynamic_slice_in_dim(log_sums, row_start, QBLOCK, 0)
        scores = band_scores(query_block, key_block, offset + row_start, seq_total)
        softmax_out = jnp.exp(scores - jnp.transpose(lse_block)[:, :, None])
        grad_probs = jnp.einsum(
            "qhd,khd->hqk", grad_block, value_block, preferred_element_type=jnp.float32
        )
        inner_sum = jnp.sum(softmax_out * grad_probs, -1, keepdims=True)
        grad_scores = (softmax_out * (grad_probs - inner_sum)).astype(jnp.bfloat16)
        query_grad = (
            jnp.einsum("hqk,khd->qhd", grad_scores, key_block, preferred_element_type=jnp.float32)
            * score_scale
        )
        key_part = (
            jnp.einsum("hqk,qhd->khd", grad_scores, query_block, preferred_element_type=jnp.float32)
            * score_scale
        )
        value_part = jnp.einsum(
            "hqk,qhd->khd",
            softmax_out.astype(jnp.bfloat16),
            grad_block,
            preferred_element_type=jnp.float32,
        )
        key_grads = lax.dynamic_update_slice_in_dim(
            key_grads,
            lax.dynamic_slice_in_dim(key_grads, row_start, key_span, 0) + key_part,
            row_start,
            0,
        )
        value_grads = lax.dynamic_update_slice_in_dim(
            value_grads,
            lax.dynamic_slice_in_dim(value_grads, row_start, key_span, 0) + value_part,
            row_start,
            0,
        )
        return ((key_grads, value_grads), query_grad)

    padded_zero = jnp.zeros(key_pad.shape, jnp.float32)
    carried, query_grads = lax.scan(
        one_block, (padded_zero, padded_zero), jnp.arange(row_count // QBLOCK, dtype=jnp.int32)
    )
    return (query_grads.reshape(queries.shape), carried[0], carried[1])


def shards(inputs, attn_gain, qkv_weight, proj_weight, mlp_gain, in_weight, out_weight, cotangent):
    gathered = (
        lax.all_gather(qkv_weight, "dp", axis=0, tiled=True),
        lax.all_gather(proj_weight, "dp", axis=0, tiled=True),
        lax.all_gather(in_weight, "dp", axis=0, tiled=True),
        lax.all_gather(out_weight, "dp", axis=0, tiled=True),
        lax.all_gather(attn_gain, "dp", axis=0, tiled=True),
        lax.all_gather(mlp_gain, "dp", axis=0, tiled=True),
    )
    qkv_full, proj_full, in_full, out_full, attn_full, mlp_full = gathered
    tokens = inputs.shape[0]
    seq_count = lax.axis_size("seq")
    seq_total = tokens * seq_count
    offset = lax.axis_index("seq") * tokens
    local_heads = HEADS // seq_count
    residual = inputs.astype(jnp.float32)
    normed_one, norm_one_back = jax.vjp(layer_norm, residual, attn_full.astype(jnp.float32))
    normed_low = normed_one.astype(jnp.bfloat16)
    projected = jnp.dot(normed_low, qkv_full, preferred_element_type=jnp.float32)
    positions = (offset + jnp.arange(tokens, dtype=jnp.int32)).astype(jnp.float32)
    cosine_table, sine_table = rotary_tables(positions, HEAD_DIM)

    def turn_pair(raw_pairs):
        return rotate(raw_pairs.reshape(tokens, 2 * HEADS, HEAD_DIM), cosine_table, sine_table)

    turned, turn_back = jax.vjp(turn_pair, projected[:, : 2 * D])
    query_low = turned[:, :HEADS].reshape(tokens, D).astype(jnp.bfloat16)
    key_low = turned[:, HEADS:].reshape(tokens, D).astype(jnp.bfloat16)
    value_low = projected[:, 2 * D :].astype(jnp.bfloat16)
    stacked = jnp.stack([query_low, key_low, value_low], 1)
    by_heads = lax.all_to_all(stacked, "seq", split_axis=2, concat_axis=0, tiled=True)
    head_queries = by_heads[:, 0].reshape(seq_total, local_heads, HEAD_DIM)
    keys_padded = jnp.pad(
        by_heads[:, 1].reshape(seq_total, local_heads, HEAD_DIM), ((WINDOW, WINDOW), (0, 0), (0, 0))
    )
    values_padded = jnp.pad(
        by_heads[:, 2].reshape(seq_total, local_heads, HEAD_DIM), ((WINDOW, WINDOW), (0, 0), (0, 0))
    )
    attended, log_sums = band_forward(head_queries, keys_padded, values_padded, 0, seq_total)
    attended_low = attended.astype(jnp.bfloat16).reshape(seq_total, D // seq_count)
    mixed_low = lax.all_to_all(attended_low, "seq", split_axis=0, concat_axis=1, tiled=True)
    attn_out = jnp.dot(mixed_low, proj_full, preferred_element_type=jnp.float32)
    hidden_state = residual + attn_out
    normed_two, norm_two_back = jax.vjp(layer_norm, hidden_state, mlp_full.astype(jnp.float32))
    normed_two_low = normed_two.astype(jnp.bfloat16)
    up_values = jnp.dot(normed_two_low, in_full, preferred_element_type=jnp.float32)
    gated, gated_back = jax.vjp(gated_gelu, up_values)
    gated_low = gated.astype(jnp.bfloat16)
    result = hidden_state + jnp.dot(gated_low, out_full, preferred_element_type=jnp.float32)
    output = result.astype(jnp.bfloat16)
    grad_result = cotangent.astype(jnp.float32)
    out_grad = jnp.einsum("tf,td->fd", gated_low, cotangent, preferred_element_type=jnp.float32)
    gated_grad = jnp.einsum("td,fd->tf", cotangent, out_full, preferred_element_type=jnp.float32)
    up_grad = gated_back(gated_grad)[0]
    up_low = up_grad.astype(jnp.bfloat16)
    in_grad = jnp.einsum("td,tf->df", normed_two_low, up_low, preferred_element_type=jnp.float32)
    normed_two_grad = jnp.einsum("tf,df->td", up_low, in_full, preferred_element_type=jnp.float32)
    hidden_part, mlp_gain_grad = norm_two_back(normed_two_grad)
    hidden_grad = grad_result + hidden_part
    attn_low = hidden_grad.astype(jnp.bfloat16)
    proj_grad = jnp.einsum("te,td->ed", mixed_low, attn_low, preferred_element_type=jnp.float32)
    mixed_grad = jnp.einsum(
        "td,ed->te", attn_low, proj_full, preferred_element_type=jnp.float32
    ).astype(jnp.bfloat16)
    grad_heads = lax.all_to_all(mixed_grad, "seq", split_axis=1, concat_axis=0, tiled=True)
    grad_heads = grad_heads.reshape(seq_total, local_heads, HEAD_DIM)
    query_grad, key_pad_grad, value_pad_grad = band_backward(
        head_queries, keys_padded, values_padded, grad_heads, log_sums, 0, seq_total
    )
    head_grads = jnp.stack(
        [
            query_grad.reshape(seq_total, D // seq_count),
            key_pad_grad[WINDOW : WINDOW + seq_total].reshape(seq_total, D // seq_count),
            value_pad_grad[WINDOW : WINDOW + seq_total].reshape(seq_total, D // seq_count),
        ],
        1,
    ).astype(jnp.bfloat16)
    token_grads = lax.all_to_all(head_grads, "seq", split_axis=0, concat_axis=2, tiled=True)
    rotated_grad = jnp.concatenate(
        [
            token_grads[:, 0].reshape(tokens, HEADS, HEAD_DIM),
            token_grads[:, 1].reshape(tokens, HEADS, HEAD_DIM),
        ],
        1,
    ).astype(jnp.float32)
    raw_grad = turn_back(rotated_grad)[0]
    proj_in_grad = jnp.concatenate([raw_grad, token_grads[:, 2].astype(jnp.float32)], 1).astype(
        jnp.bfloat16
    )
    qkv_grad = jnp.einsum("td,tf->df", normed_low, proj_in_grad, preferred_element_type=jnp.float32)
    normed_grad = jnp.einsum(
        "tf,df->td", proj_in_grad, qkv_full, preferred_element_type=jnp.float32
    )
    input_part, attn_gain_grad = norm_one_back(normed_grad)
    input_grad = (hidden_grad + input_part).astype(jnp.bfloat16)
    shares = (
        lax.psum_scatter(qkv_grad, "dp", scatter_dimension=0, tiled=True),
        lax.psum_scatter(proj_grad, "dp", scatter_dimension=0, tiled=True),
        lax.psum_scatter(in_grad, "dp", scatter_dimension=0, tiled=True),
        lax.psum_scatter(out_grad, "dp", scatter_dimension=0, tiled=True),
        lax.psum_scatter(attn_gain_grad, "dp", scatter_dimension=0, tiled=True),
        lax.psum_scatter(mlp_gain_grad, "dp", scatter_dimension=0, tiled=True),
    )
    totals = (
        lax.psum(shares[0].astype(jnp.bfloat16), "seq").astype(jnp.float32),
        lax.psum(shares[1].astype(jnp.bfloat16), "seq").astype(jnp.float32),
        lax.psum(shares[2].astype(jnp.bfloat16), "seq").astype(jnp.float32),
        lax.psum(shares[3].astype(jnp.bfloat16), "seq").astype(jnp.float32),
        lax.psum(shares[4].astype(jnp.bfloat16), "seq").astype(jnp.float32),
        lax.psum(shares[5].astype(jnp.bfloat16), "seq").astype(jnp.float32),
    )
    return (output, input_grad, totals[4], totals[0], totals[1], totals[5], totals[2], totals[3])


def solution(mesh):
    in_specs = (
        P(("dp", "seq"), None),
        P("dp"),
        P("dp", None),
        P("dp", None),
        P("dp"),
        P("dp", None),
        P("dp", None),
        P(("dp", "seq"), None),
    )
    out_specs = (
        P(("dp", "seq"), None),
        P(("dp", "seq"), None),
        P("dp"),
        P("dp", None),
        P("dp", None),
        P("dp"),
        P("dp", None),
        P("dp", None),
    )
    return jax.shard_map(shards, mesh=mesh, in_specs=in_specs, out_specs=out_specs, check_vma=False)
```

profile of v0, /device:TPU:0, one launch (start us, length us, event | category | flops | bytes accessed | tf_op | source)
XLA Modules:
  0.0 997.3 jit_solution(2272519886768296588)
XLA Ops:
  11.6 15.3 %all-reduce.11 = (bf16[768]{0:T(1024)(128)(2,1)S(1)}, bf16[768]{0:T(1024)(128)(2,1)S(1)}) all-reduce(bf16[768]{0:T(1024)(128)(2,1)S(1)} %dynamic-update-slice, bf16[768]{0:T(1024)(128)(2,1)S(1)} %dynamic-update-slice.1), channel_id=1, replica_groups=mesh['dp'=8,'seq'=4] {'dp'}, use_global_device_ids=true, to_apply=%add.6 | all-reduce | flops 1536 | bytes 6144
  29.0 17.7 %all-gather.5.cloned.1.call-done = bf16[768,2304]{1,0:T(8,128)(2,1)} async-done(((bf16[96,2304]{1,0:T(8,128)(2,1)}), bf16[768,2304]{1,0:T(8,128)(2,1)}) %all-gather.5.cloned.1.call-update) | async-done | bytes 3538960 | tf_op jit(solution)/shard_map/all_gather | solution.py:138
  46.7 6.2 fusion.81
  56.7 6.6 copy.55
  80.8 11.1 %copy.58 = bf16[1024,3,768]{0,1,2:T(4,128)(2,1)} copy(bf16[1024,3,768]{2,0,1:T(8,128)(2,1)} %pad_maximum_fusion) | data formatting | bytes 9437184 | tf_op jit(solution)/shard_map/stack | solution.py:165
  91.9 5.2 all-to-all-start
  98.6 137.3 %all-to-all-done = bf16[1024,3,768]{0,1,2:T(4,128)(2,1)} async-done(((bf16[1024,3,768]{0,1,2:T(4,128)(2,1)}), bf16[1024,3,768]{0,1,2:T(4,128)(2,1)}, u32[]{:S(2)}, u32[]{:S(2)}) %all-to-all-start) | async-done | bytes 4718624 | tf_op jit(solution)/shard_map/all_to_all | solution.py:166
  236.0 4.7 copy.59
  246.6 67.9 %while.30 = (s32[]{:T(128)}, bf16[8,512,3,64]{1,3,2,0:T(8,128)(2,1)}, f32[8,512,3]{1,2,0:T(4,128)}, s32[8]{0:T(128)S(1)}, bf16[4224,3,64]{0,2,1:T(8,128)(2,1)}, ...) while((s32[]{:T(128)}, ...), condition=%wide.region_5.6_spmd, body=%wide.region_2.5_spmd.sunk | while | flops 265094656 | bytes 14252788 | solution.py:77
  324.6 4.4 all-to-all-start.1
  332.6 33.3 %all-to-all-done.1 = bf16[4,1024,192]{1,2,0:T(8,128)(2,1)} async-done(((bf16[4,1024,192]{1,2,0:T(8,128)(2,1)}), bf16[4,1024,192]{1,2,0:T(8,128)(2,1)}, u32[]{:S(2)}, u32[]{:S(2)}) %all-to-all-start.1) | async-done | bytes 1572896 | tf_op jit(solution)/shard_map/all_to_all | solution.py:176
  371.3 10.7 %fusion.89 = f32[1024,2304]{1,0:T(8,128)} fusion(bf16[768,2304]{1,0:T(8,128)(2,1)} %all-gather.9.cloned.1.call-done, f32[1024,768]{0,1:T(8,128)} %copy-done.6, f32[768]{0:T(1024)S(1)} %convert_element_type.148, f32[1024]{0:T(1024)S(1)} %fusion.84, f32[1024]{0:T(1024)S(1)} %broadcast_multiply_fusion), kind=kOutput, calls=%fused_computation.152 | convolution fusion | flops 3627024384 | bytes 16133120 | tf_op jit(solution)/shard_map/dot_general | solution.py:181
  382.0 14.9 %fusion.76 = (f32[1024,1152]{1,0:T(8,128)}, f32[1024,1152]{1,0:T(8,128)S(1)}, f32[1024,1152]{1,0:T(8,128)S(1)}) fusion(f32[1024,2304]{1,0:T(8,128)} %fusion.89, bf16[1024,768]{1,0:T(8,128)(2,1)S(1)} %copy-done.15, bf16[1152,768]{1,0:T(8,128)(2,1)} %all-gather.11.cloned.1.call-done), kind=kOutput, calls=%fused_computation.125 | convolution fusion | flops 1888616448 | bytes 22216704 | tf_op jit(solution)/shard_map/td,fd->tf/dot_general | solution.py:188
  400.4 9.0 multiply_reduce_fusion.1
  413.0 4.3 fusion.98
  417.4 5.6 fusion.99
  432.0 11.4 %fusion.77 = f32[768,2304]{1,0:T(8,128)} fusion(f32[1024,1152]{1,0:T(8,128)} %copy-done.9, f32[1024,1152]{1,0:T(8,128)} %get-tuple-element.312, f32[1024,768]{0,1:T(8,128)} %copy-done.6, f32[768]{0:T(1024)S(1)} %convert_element_type.148, f32[1024]{0:T(1024)S(1)} %fusion.84, f32[1024]{0:T(1024)S(1)} %broadcast_multiply_fusion), kind=kOutput, calls=%fused_computation.126 | convolution fusion | flops 3631742976 | bytes 19672064 | tf_op jit(solution)/shard_map/td,tf->df/dot_general | solution.py:191
  443.5 24.9 %all-to-all-done.2 = bf16[1024,4,192]{0,2,1:T(8,128)(2,1)S(1)} async-done(((bf16[1024,4,192]{0,2,1:T(8,128)(2,1)}), bf16[1024,4,192]{0,2,1:T(8,128)(2,1)S(1)}, u32[]{:S(2)}, u32[]{:S(2)}) %all-to-all-start.2) | async-done | bytes 1572896 | tf_op jit(solution)/shard_map/all_to_all | solution.py:200
  479.1 134.9 %while.31 = (s32[]{:T(128)}, f32[4224,3,64]{0,2,1:T(8,128)}, f32[4224,3,64]{0,2,1:T(8,128)}, bf16[8,512,3,64]{1,3,2,0:T(8,128)(2,1)}, s32[8]{0:T(128)S(1)}, /*in...) while((s32[]{:T(128)}, f32[4224,3,64]{0,2,1:T(8,128)}, ...), condition=%wide.region_12.13_spmd, body=%wide.region_10.12_spmd.sunk | while | flops 640099840 | bytes 49803588 | solution.py:130
  518.7 4.2 multiply_reduce_fusion.5
  535.8 4.1 multiply_reduce_fusion.5
  624.4 12.8 %copy.67 = bf16[4096,3,192]{2,1,0:T(4,128)(2,1)} copy(bf16[4096,3,192]{0,2,1:T(8,128)(2,1)} %pad_maximum_fusion.1) | data formatting | bytes 9437184 | tf_op jit(solution)/shard_map/stack | solution.py:205
  637.2 190.6 %all_to_all.68 = bf16[4096,3,192]{2,1,0:T(4,128)(2,1)} all-to-all(bf16[4096,3,192]{2,1,0:T(4,128)(2,1)} %copy.67), channel_id=1, replica_groups=mesh['dp'=8,'seq'=4] {'seq'}, dimensions={0} | all-to-all | bytes 9437184 | tf_op jit(solution)/shard_map/all_to_all | solution.py:213
  827.8 12.8 %copy.69 = bf16[1024,3,4,192]{0,3,2,1:T(8,128)(2,1)} copy(bf16[1024,3,4,192]{3,1,0,2:T(4,128)(2,1)} %bitcast.117) | data formatting | bytes 9437184 | tf_op jit(solution)/shard_map/all_to_all | solution.py:213
  848.8 7.7 fusion.72
  857.2 6.7 add_convert_fusion.2
  870.4 8.6 fusion.71
  881.4 38.9 %reduce-scatter.5.cloned.1.call-done = f32[96,2304]{1,0:T(8,128)} async-done(((f32[768,2304]{1,0:T(8,128)}), f32[96,2304]{1,0:T(8,128)}) %reduce-scatter.5.cloned.1.call-update) | async-done | bytes 884752 | tf_op jit(solution)/shard_map/reduce_scatter | solution.py:232
  925.6 13.4 %all-reduce.10 = (bf16[768]{0:T(1024)(128)(2,1)S(1)}, bf16[768]{0:T(1024)(128)(2,1)S(1)}) all-reduce(f32[768]{0:T(1024)S(1)} %get-tuple-element.264, f32[768]{0:T(1024)S(1)} %get-tuple-element.262), channel_id=2, replica_groups=mesh['dp'=8,'seq'=4] {'dp'}, use_global_device_ids=true, to_apply=%region_16.17.clone | all-reduce | flops 1536 | bytes 9216
  939.1 12.3 %all-reduce.12 = (bf16[96]{0:T(256)(128)(2,1)S(1)}, bf16[96]{0:T(256)(128)(2,1)S(1)}) all-reduce(bf16[96]{0:T(256)(128)(2,1)S(1)} %dynamic-slice.9, bf16[96]{0:T(256)(128)(2,1)S(1)} %dynamic-slice.8), channel_id=1, replica_groups=mesh['dp'=8,'seq'=4] {'seq'}, use_global_device_ids=true, to_apply=%region_17.18 | all-reduce | flops 192 | bytes 768 | tf_op jit(solution)/shard_map/psum | solution.py:244
  952.4 5.5 add_convert_fusion.1
  960.5 23.2 %all-reduce.16.cloned.1.call-done = (bf16[96,2304]{1,0:T(8,128)(2,1)}, bf16[96,768]{1,0:T(8,128)(2,1)}, bf16[96,2304]{1,0:T(8,128)(2,1)}, bf16[144,768]{1,0:T(8,128)(2,1)}) async-done(((bf16[96,2304]{1,0:T(8,128)(2,1)}, bf16[96,768]{1,0:T(8,128)(2,1)}, bf16[96,2304]{1,0:T(8,128)(2,1)}, bf16[144,768]{1,0:T(8,128)(2,1)}), (bf16[96,2304]{1,0:T(8,128)(2,1)}, bf16[96,768]{1,0:T(8,128)(2,1)}, ...) | async-done | bytes 1253392 | tf_op jit(solution)/shard_map/psum | solution.py:240
  (347 shorter events, 307.2 us)
Async XLA Ops:
  7.2 4.1 copy-start.29
  7.2 39.5 %all-gather.5.cloned.1.call-start = ((), (), s32[]{:S(2)}) async-start(), calls=%async_computation.8 | async-start | bytes 3981312 | tf_op jit(solution)/shard_map/all_gather | solution.py:138
  9.7 356.2 %copy-start.1 = (bf16[1024,768]{0,1:T(8,128)(2,1)}, bf16[1024,768]{0,1:T(8,128)(2,1)S(1)}, u32[]{:S(2)}) copy-start(bf16[1024,768]{0,1:T(8,128)(2,1)S(1)} %copy.54) | copy-start | bytes 4718596
  26.9 26.0 %copy-start.21 = (f32[768]{0:T(1024)}, f32[768]{0:T(1024)S(1)}, u32[]{:S(2)}) copy-start(f32[768]{0:T(1024)S(1)} %convert_element_type.141) | copy-start | bytes 9220
  28.2 38.7 %copy-start.11 = (f32[1024,64]{0,1:T(8,128)}, f32[1024,64]{0,1:T(8,128)S(1)}, u32[]{:S(2)}) copy-start(f32[1024,64]{0,1:T(8,128)S(1)} %get-tuple-element.346) | copy-start | bytes 786436
  28.5 24.4 %copy-start.19 = (f32[1024]{0:T(1024)}, f32[1024]{0:T(1024)S(1)}, u32[]{:S(2)}) copy-start(f32[1024]{0:T(1024)S(1)} %broadcast_multiply_fusion.1) | copy-start | bytes 12292
  29.0 23.9 %copy-start.25 = (f32[1024]{0:T(1024)}, f32[1024]{0:T(1024)S(1)}, u32[]{:S(2)}) copy-start(f32[1024]{0:T(1024)S(1)} %fusion.70) | copy-start | bytes 12292
  29.0 23.9 %copy-start.23 = (f32[1024]{0:T(1024)}, f32[1024]{0:T(1024)S(1)}, u32[]{:S(2)}) copy-start(f32[1024]{0:T(1024)S(1)} %fusion.83) | copy-start | bytes 12292
  63.2 4.0 slice-start
  63.2 4.7 slice-start.1
  63.2 4.7 copy-start.13
  91.9 144.1 %all-to-all-start = ((bf16[1024,3,768]{0,1,2:T(4,128)(2,1)}), bf16[1024,3,768]{0,1,2:T(4,128)(2,1)}, u32[]{:S(2)}, u32[]{:S(2)}) async-start(bf16[1024,3,768]{0,1,2:T(4,128)(2,1)} %copy.58), calls=%async_computation | async-start | bytes 12582912 | tf_op jit(solution)/shard_map/all_to_all | solution.py:166
  97.1 235.5 %all-gather.7.cloned.1.call-start = ((), (), s32[]{:S(2)}) async-start(), calls=%async_computation.9 | async-start | bytes 1327104 | tf_op jit(solution)/shard_map/all_gather | solution.py:139
  97.9 273.4 %all-gather.9.cloned.1.call-start = ((), (), s32[]{:S(2)}) async-start(), calls=%async_computation.10 | async-start | bytes 3981312 | tf_op jit(solution)/shard_map/all_gather | solution.py:140
  324.6 41.3 %all-to-all-start.1 = ((bf16[4,1024,192]{1,2,0:T(8,128)(2,1)}), bf16[4,1024,192]{1,2,0:T(8,128)(2,1)}, u32[]{:S(2)}, u32[]{:S(2)}) async-start(bf16[4,1024,192]{1,2,0:T(8,128)(2,1)} %copy.62), calls=%async_computation.1 | async-start | bytes 3145728 | tf_op jit(solution)/shard_map/all_to_all | solution.py:176
  329.0 53.1 %all-gather.11.cloned.1.call-start = ((), (), s32[]{:S(2)}) async-start(), calls=%async_computation.11 | async-start | bytes 1990656 | tf_op jit(solution)/shard_map/all_gather | solution.py:141
  329.5 537.4 %reduce-scatter.7.cloned.1.call-start = ((), (), s32[]{:S(2)}) async-start(), calls=%async_computation.13 | async-start | bytes 2654208 | tf_op jit(solution)/shard_map/reduce_scatter | solution.py:233
  371.3 10.8 %copy-start.15 = (bf16[1024,768]{1,0:T(8,128)(2,1)S(1)}, bf16[1024,768]{1,0:T(8,128)(2,1)}, u32[]{:S(2)}) copy-start(bf16[1024,768]{1,0:T(8,128)(2,1)} %param.19) | copy-start | bytes 4718596
  382.0 14.9 %copy-start.8 = (f32[1024,2304]{1,0:T(8,128)S(1)}, f32[1024,2304]{1,0:T(8,128)}, u32[]{:S(2)}) copy-start(f32[1024,2304]{1,0:T(8,128)} %fusion.89) | copy-start | bytes 28311556
  400.4 9.0 copy-start.9
  417.3 451.3 %reduce-scatter.11.cloned.1.call-start = ((), (), s32[]{:S(2)}) async-start(), calls=%async_computation.15 | async-start | bytes 3981312 | tf_op jit(solution)/shard_map/reduce_scatter | solution.py:235
  428.4 40.0 %all-to-all-start.2 = ((bf16[1024,4,192]{0,2,1:T(8,128)(2,1)}), bf16[1024,4,192]{0,2,1:T(8,128)(2,1)S(1)}, u32[]{:S(2)}, u32[]{:S(2)}) async-start(bf16[1024,4,192]{0,2,1:T(8,128)(2,1)} %bitcast.135), calls=%async_computation.2 | async-start | bytes 3145728 | tf_op jit(solution)/shard_map/all_to_all | solution.py:200
  431.9 447.2 %reduce-scatter.9.cloned.1.call-start = ((), (), s32[]{:S(2)}) async-start(), calls=%async_computation.14 | async-start | bytes 7962624 | tf_op jit(solution)/shard_map/reduce_scatter | solution.py:234
  443.4 476.9 %reduce-scatter.5.cloned.1.call-start = ((), (), s32[]{:S(2)}) async-start(), calls=%async_computation.12 | async-start | bytes 7962624 | tf_op jit(solution)/shard_map/reduce_scatter | solution.py:232
  502.0 4.0 copy-start
  518.7 4.2 copy-start
  535.8 4.5 copy-start
  569.8 4.0 copy-start
  856.5 127.2 %all-reduce.16.cloned.1.call-start = ((), (), s32[]{:S(2)}) async-start(), calls=%async_computation.16 | async-start | bytes 2506752 | tf_op jit(solution)/shard_map/psum | solution.py:240
  870.4 8.6 copy-start.26
  922.3 30.1 %copy-start.5 = (bf16[1024,768]{0,1:T(8,128)(2,1)S(1)}, bf16[1024,768]{0,1:T(8,128)(2,1)}, u32[]{:S(2)}) copy-start(bf16[1024,768]{0,1:T(8,128)(2,1)} %copy.64) | copy-start | bytes 4718596
  983.8 5.7 copy-start.18
  (19 other events, 52.0 us)
Sparse Core Ops, SparseCore 0:
  9.9 36.7 all-gather.4
  99.8 24.4 all-gather.6
  126.3 33.9 all-gather.8
  331.4 26.9 all-gather.10
  417.5 40.6 reduce-scatter.6
  461.8 48.0 reduce-scatter.10
  513.9 65.5 reduce-scatter.8
  856.7 63.5 reduce-scatter.4
  923.7 59.9 all-reduce.15
where the time goes:
time: 1010 us; the launch traced here: 997 us
  waiting for transfers between devices  278 us (28%)
  matrix products  244 us (24%)
  blocking collectives  232 us (23%)
  local copies, waits for them, and re-layouts  131 us (13%)
  other arithmetic  72 us (7%)
  between operations  16.2 us (2%)
  starting transfers between devices  14.1 us (1%)
  loops' own time  10.6 us (1%)
    all_to_all x1, blocking collectives, shards(): lax.all_to_all(head_grads, 'seq', split_axis=0, concat_axis=2, tiled=True)  191 us
    all_to_all x1, waiting for transfers between devices, shards(): lax.all_to_all(stacked, 'seq', split_axis=2, concat_axis=0, tiled=True)  137 us
    dot_general x16, matrix products, band_scores(): jnp.einsum('qhd,khd->hqk', query_block, key_block, preferred_element_type...  48.2 us
    reduce_scatter x1, waiting for transfers between devices, shards(): lax.psum_scatter(qkv_grad, 'dp', scatter_dimension=0, tiled=True)  38.9 us
    all_to_all x1, waiting for transfers between devices, shards(): lax.all_to_all(attended_low, 'seq', split_axis=0, concat_axis=1, tiled=True)  33.3 us
    unnamed x2, blocking collectives  28.7 us
    dot_general x8, matrix products, one_block(): jnp.einsum('qhd,khd->hqk', grad_block, value_block, preferred_element_typ...  28.3 us
    dot_general x8, matrix products, one_block(): jnp.einsum('hqk,khd->qhd', softmax_low, value_block, preferred_element_ty...  25.1 us
  transfers between devices with their start and end apart: 12, of which 6 were waited for; matrix products, arithmetic and copies ran while one was open for 35% of the time, Pallas kernels for 0%

commit v1 on v0

--- a/solution.py
+++ b/solution.py
@@ -12,6 +12,28 @@
 epsilon = 1e-05
 theta_base = 10000.0
 masked_score = -1e30
+
+
+def cut_along(array, dim, devices):
+    before, after = (array.shape[:dim], array.shape[dim + 1 :])
+    return jnp.moveaxis(array.reshape(*before, devices, -1, *after), dim, 0)
+
+
+def in_order(blocks, dim):
+    blocks = jnp.moveaxis(blocks, 0, dim)
+    shape = blocks.shape
+    return blocks.reshape(*shape[:dim], shape[dim] * shape[dim + 1], *shape[dim + 2 :])
+
+
+def sent_to_each(x, axis, split_dim, concat_dim):
+    size, mine = (lax.axis_size(axis), lax.axis_index(axis))
+    tiles = cut_along(x, split_dim, size)
+    outs = [tiles[mine]]
+    for turn in range(1, size):
+        sent = tiles[(mine + turn) % size]
+        outs.append(lax.ppermute(sent, axis, [(i, (i + turn) % size) for i in range(size)]))
+    tiles = jnp.stack(outs)[(mine - jnp.arange(size)) % size]
+    return in_order(tiles, concat_dim)
 
 
 def layer_norm(features, gain_vector):
@@ -210,7 +232,7 @@
         ],
         1,
     ).astype(jnp.bfloat16)
-    token_grads = lax.all_to_all(head_grads, "seq", split_axis=0, concat_axis=2, tiled=True)
+    token_grads = sent_to_each(head_grads, "seq", 0, 2)
     rotated_grad = jnp.concatenate(
         [
             token_grads[:, 0].reshape(tokens, HEADS, HEAD_DIM),

time: 1010 us -> 913 us (0.904)
  blocking collectives: 232 us -> 41 us
  waiting for transfers between devices: 278 us -> 378 us
    all_to_all x1 -> x0, blocking collectives: 191 us -> none  [shards(): lax.all_to_all(head_grads, 'seq', split_axis=0, concat_axis=2, tiled=True)]
    ppermute x0 -> x3, waiting for transfers between devices: none -> 75.8 us  [sent_to_each(): lax.ppermute(sent, axis, [(i, (i + turn) % size) for i in range(size)])]
    reduce_scatter x1, waiting for transfers between devices: 38.9 us -> 63.2 us  [shards(): lax.psum_scatter(qkv_grad, 'dp', scatter_dimension=0, tiled=True)]
    all_to_all x1 -> x0, local copies, waits for them, and re-layouts: 12.8 us -> none  [shards(): lax.all_to_all(head_grads, 'seq', split_axis=0, concat_axis=2, tiled=True)]
    unnamed x73 -> x77, local copies, waits for them, and re-layouts: 19.4 us -> 21.1 us
  transfers between devices with their start and end apart: 12 -> 15, of which waited for: 6 -> 8; matrix products, arithmetic and copies ran while one was open for 35% -> 38% of each run, Pallas kernels for 0% -> 0%
where the time goes in v1:
time: 913 us; the launch traced here: 901 us
  waiting for transfers between devices  378 us (41%)
  matrix products  244 us (27%)
  local copies, waits for them, and re-layouts  123 us (13%)
  other arithmetic  71.3 us (8%)
  blocking collectives  41 us (4%)
  starting transfers between devices  18.1 us (2%)
  between operations  16 us (2%)
  loops' own time  9.83 us (1%)
    all_to_all x1, waiting for transfers between devices, shards(): lax.all_to_all(stacked, 'seq', split_axis=2, concat_axis=0, tiled=True)  137 us
    ppermute x3, waiting for transfers between devices, sent_to_each(): lax.ppermute(sent, axis, [(i, (i + turn) % size) for i in range(size)])  75.8 us
    reduce_scatter x1, waiting for transfers between devices, shards(): lax.psum_scatter(qkv_grad, 'dp', scatter_dimension=0, tiled=True)  63.2 us
    dot_general x16, matrix products, band_scores(): jnp.einsum('qhd,khd->hqk', query_block, key_block, preferred_element_type...  48.5 us
    all_to_all x1, waiting for transfers between devices, shards(): lax.all_to_all(attended_low, 'seq', split_axis=0, concat_axis=1, tiled=True)  33.5 us
    dot_general x8, matrix products, one_block(): jnp.einsum('qhd,khd->hqk', grad_block, value_block, preferred_element_typ...  28.8 us
    unnamed x2, blocking collectives  28.7 us
    dot_general x8, matrix products, one_block(): jnp.einsum('hqk,khd->qhd', softmax_low, value_block, preferred_element_ty...  25.1 us
  transfers between devices with their start and end apart: 15, of which 8 were waited for; matrix products, arithmetic and copies ran while one was open for 38% of the time, Pallas kernels for 0%

profile of v1, /device:TPU:0, one launch (start us, length us, event | category | flops | bytes accessed | tf_op | source)
XLA Modules:
  0.0 901.4 jit_solution(8948427698868536293)
XLA Ops:
  11.6 15.3 %all-reduce.11 = (bf16[768]{0:T(1024)(128)(2,1)S(1)}, bf16[768]{0:T(1024)(128)(2,1)S(1)}) all-reduce(bf16[768]{0:T(1024)(128)(2,1)S(1)} %dynamic-update-slice, bf16[768]{0:T(1024)(128)(2,1)S(1)} %dynamic-update-slice.1), channel_id=1, replica_groups=mesh['dp'=8,'seq'=4] {'dp'}, use_global_device_ids=true, to_apply=%add.6 | all-reduce | flops 1536 | bytes 6144
  29.0 17.7 %all-gather.5.cloned.1.call-done = bf16[768,2304]{1,0:T(8,128)(2,1)} async-done(((bf16[96,2304]{1,0:T(8,128)(2,1)}), bf16[768,2304]{1,0:T(8,128)(2,1)}) %all-gather.5.cloned.1.call-update) | async-done | bytes 3538960 | tf_op jit(solution)/shard_map/all_gather | solution.py:160
  46.7 6.2 fusion.81
  56.7 6.6 copy.57
  80.8 11.1 %copy.60 = bf16[1024,3,768]{0,1,2:T(4,128)(2,1)} copy(bf16[1024,3,768]{2,0,1:T(8,128)(2,1)} %pad_maximum_fusion) | data formatting | bytes 9437184 | tf_op jit(solution)/shard_map/stack | solution.py:187
  91.8 5.3 all-to-all-start
  98.7 137.3 %all-to-all-done = bf16[1024,3,768]{0,1,2:T(4,128)(2,1)} async-done(((bf16[1024,3,768]{0,1,2:T(4,128)(2,1)}), bf16[1024,3,768]{0,1,2:T(4,128)(2,1)}, u32[]{:S(2)}, u32[]{:S(2)}) %all-to-all-start) | async-done | bytes 4718624 | tf_op jit(solution)/shard_map/all_to_all | solution.py:188
  236.0 4.7 copy.61
  246.6 68.3 %while.30 = (s32[]{:T(128)}, bf16[8,512,3,64]{1,3,2,0:T(8,128)(2,1)}, f32[8,512,3]{1,2,0:T(4,128)}, s32[8]{0:T(128)S(1)}, bf16[4224,3,64]{0,2,1:T(8,128)(2,1)}, ...) while((s32[]{:T(128)}, ...), condition=%wide.region_5.6_spmd, body=%wide.region_2.5_spmd.sunk | while | flops 265094656 | bytes 14252788 | solution.py:99
  325.1 4.3 all-to-all-start.1
  332.9 33.5 %all-to-all-done.1 = bf16[4,1024,192]{1,2,0:T(8,128)(2,1)} async-done(((bf16[4,1024,192]{1,2,0:T(8,128)(2,1)}), bf16[4,1024,192]{1,2,0:T(8,128)(2,1)}, u32[]{:S(2)}, u32[]{:S(2)}) %all-to-all-start.1) | async-done | bytes 1572896 | tf_op jit(solution)/shard_map/all_to_all | solution.py:198
  371.8 10.7 %fusion.91 = f32[1024,2304]{1,0:T(8,128)} fusion(bf16[768,2304]{1,0:T(8,128)(2,1)} %all-gather.9.cloned.1.call-done, f32[1024,768]{0,1:T(8,128)} %copy-done.6, f32[768]{0:T(1024)S(1)} %convert_element_type.149, f32[1024]{0:T(1024)S(1)} %fusion.84, f32[1024]{0:T(1024)S(1)} %broadcast_multiply_fusion), kind=kOutput, calls=%fused_computation.167 | convolution fusion | flops 3627024384 | bytes 16133120 | tf_op jit(solution)/shard_map/dot_general | solution.py:203
  382.5 14.9 %fusion.76 = (f32[1024,1152]{1,0:T(8,128)}, f32[1024,1152]{1,0:T(8,128)S(1)}, f32[1024,1152]{1,0:T(8,128)S(1)}) fusion(f32[1024,2304]{1,0:T(8,128)} %fusion.91, bf16[1024,768]{1,0:T(8,128)(2,1)S(1)} %copy-done.16, bf16[1152,768]{1,0:T(8,128)(2,1)} %all-gather.11.cloned.1.call-done), kind=kOutput, calls=%fused_computation.129 | convolution fusion | flops 1888616448 | bytes 22216704 | tf_op jit(solution)/shard_map/td,fd->tf/dot_general | solution.py:210
  401.0 9.0 multiply_reduce_fusion.1
  413.6 4.2 fusion.100
  417.9 5.5 fusion.101
  432.5 11.5 %fusion.77 = f32[768,2304]{1,0:T(8,128)} fusion(f32[1024,1152]{1,0:T(8,128)} %copy-done.10, f32[1024,1152]{1,0:T(8,128)} %get-tuple-element.312, f32[1024,768]{0,1:T(8,128)} %copy-done.6, f32[768]{0:T(1024)S(1)} %convert_element_type.149, f32[1024]{0:T(1024)S(1)} %fusion.84, f32[1024]{0:T(1024)S(1)} %broadcast_multiply_fusion), kind=kOutput, calls=%fused_computation.133 | convolution fusion | flops 3631742976 | bytes 19672064 | tf_op jit(solution)/shard_map/td,tf->df/dot_general | solution.py:213
  444.0 24.7 %all-to-all-done.2 = bf16[1024,4,192]{0,2,1:T(8,128)(2,1)S(1)} async-done(((bf16[1024,4,192]{0,2,1:T(8,128)(2,1)}), bf16[1024,4,192]{0,2,1:T(8,128)(2,1)S(1)}, u32[]{:S(2)}, u32[]{:S(2)}) %all-to-all-start.2) | async-done | bytes 1572896 | tf_op jit(solution)/shard_map/all_to_all | solution.py:222
  479.5 134.3 %while.31 = (s32[]{:T(128)}, f32[4224,3,64]{0,2,1:T(8,128)}, f32[4224,3,64]{0,2,1:T(8,128)}, bf16[8,512,3,64]{1,3,2,0:T(8,128)(2,1)}, s32[8]{0:T(128)S(1)}, /*in...) while((s32[]{:T(128)}, f32[4224,3,64]{0,2,1:T(8,128)}, ...), condition=%wide.region_12.13_spmd, body=%wide.region_10.12_spmd.sunk | while | flops 640099840 | bytes 49803588 | solution.py:152
  502.2 4.1 multiply_reduce_fusion.5
  518.9 4.6 multiply_reduce_fusion.5
  637.4 26.9 %collective-permute-done = bf16[1024,3,192]{0,2,1:T(8,128)(2,1)S(1)} collective-permute-done((bf16[1024,3,192]{0,2,1:T(8,128)(2,1)S(1)}, bf16[1024,3,192]{0,2,1:T(8,128)(2,1)S(1)}, u32[]{:S(2)}, u32[]{:S(2)}) %collective-permute-start) | collective-permute-done | bytes 1179680 | tf_op jit(solution)/shard_map/ppermute | solution.py:34
  664.3 48.8 %collective-permute-done.1 = bf16[1024,3,192]{0,2,1:T(8,128)(2,1)S(1)} collective-permute-done((bf16[1024,3,192]{0,2,1:T(8,128)(2,1)S(1)}, bf16[1024,3,192]{0,2,1:T(8,128)(2,1)S(1)}, u32[]{:S(2)}, u32[]{:S(2)}) %collective-permute-start.1) | collective-permute-done | bytes 1179680 | tf_op jit(solution)/shard_map/ppermute | solution.py:34
  715.8 5.3 gather_fusion
  729.9 7.7 fusion.72
  738.3 6.5 add_convert_fusion.2
  749.2 8.5 fusion.71
  761.5 63.2 %reduce-scatter.5.cloned.1.call-done = f32[96,2304]{1,0:T(8,128)} async-done(((f32[768,2304]{1,0:T(8,128)}), f32[96,2304]{1,0:T(8,128)}) %reduce-scatter.5.cloned.1.call-update) | async-done | bytes 884752 | tf_op jit(solution)/shard_map/reduce_scatter | solution.py:254
  830.0 13.3 %all-reduce.10 = (bf16[768]{0:T(1024)(128)(2,1)S(1)}, bf16[768]{0:T(1024)(128)(2,1)S(1)}) all-reduce(f32[768]{0:T(1024)S(1)} %get-tuple-element.264, f32[768]{0:T(1024)S(1)} %get-tuple-element.262), channel_id=2, replica_groups=mesh['dp'=8,'seq'=4] {'dp'}, use_global_device_ids=true, to_apply=%region_16.17.clone | all-reduce | flops 1536 | bytes 9216
  843.5 12.3 %all-reduce.12 = (bf16[96]{0:T(256)(128)(2,1)S(1)}, bf16[96]{0:T(256)(128)(2,1)S(1)}) all-reduce(bf16[96]{0:T(256)(128)(2,1)S(1)} %dynamic-slice.9, bf16[96]{0:T(256)(128)(2,1)S(1)} %dynamic-slice.8), channel_id=1, replica_groups=mesh['dp'=8,'seq'=4] {'seq'}, use_global_device_ids=true, to_apply=%region_17.18 | all-reduce | flops 192 | bytes 768 | tf_op jit(solution)/shard_map/psum | solution.py:266
  856.8 5.5 add_convert_fusion.1
  864.9 23.3 %all-reduce.16.cloned.1.call-done = (bf16[96,2304]{1,0:T(8,128)(2,1)}, bf16[96,768]{1,0:T(8,128)(2,1)}, bf16[96,2304]{1,0:T(8,128)(2,1)}, bf16[144,768]{1,0:T(8,128)(2,1)}) async-done(((bf16[96,2304]{1,0:T(8,128)(2,1)}, bf16[96,768]{1,0:T(8,128)(2,1)}, bf16[96,2304]{1,0:T(8,128)(2,1)}, bf16[144,768]{1,0:T(8,128)(2,1)}), (bf16[96,2304]{1,0:T(8,128)(2,1)}, bf16[96,768]{1,0:T(8,128)(2,1)}, ...) | async-done | bytes 1253392 | tf_op jit(solution)/shard_map/psum | solution.py:262
  (362 shorter events, 323.1 us)
Async XLA Ops:
  7.2 4.1 copy-start.30
  7.2 39.5 %all-gather.5.cloned.1.call-start = ((), (), s32[]{:S(2)}) async-start(), calls=%async_computation.7 | async-start | bytes 3981312 | tf_op jit(solution)/shard_map/all_gather | solution.py:160
  9.7 356.7 %copy-start.1 = (bf16[1024,768]{0,1:T(8,128)(2,1)}, bf16[1024,768]{0,1:T(8,128)(2,1)S(1)}, u32[]{:S(2)}) copy-start(bf16[1024,768]{0,1:T(8,128)(2,1)S(1)} %copy.56) | copy-start | bytes 4718596
  26.9 26.0 %copy-start.22 = (f32[768]{0:T(1024)}, f32[768]{0:T(1024)S(1)}, u32[]{:S(2)}) copy-start(f32[768]{0:T(1024)S(1)} %convert_element_type.142) | copy-start | bytes 9220
  28.2 38.7 %copy-start.12 = (f32[1024,64]{0,1:T(8,128)}, f32[1024,64]{0,1:T(8,128)S(1)}, u32[]{:S(2)}) copy-start(f32[1024,64]{0,1:T(8,128)S(1)} %get-tuple-element.350) | copy-start | bytes 786436
  28.5 24.4 %copy-start.20 = (f32[1024]{0:T(1024)}, f32[1024]{0:T(1024)S(1)}, u32[]{:S(2)}) copy-start(f32[1024]{0:T(1024)S(1)} %broadcast_multiply_fusion.1) | copy-start | bytes 12292
  29.0 23.9 %copy-start.26 = (f32[1024]{0:T(1024)}, f32[1024]{0:T(1024)S(1)}, u32[]{:S(2)}) copy-start(f32[1024]{0:T(1024)S(1)} %fusion.70) | copy-start | bytes 12292
  29.0 23.9 %copy-start.24 = (f32[1024]{0:T(1024)}, f32[1024]{0:T(1024)S(1)}, u32[]{:S(2)}) copy-start(f32[1024]{0:T(1024)S(1)} %fusion.83) | copy-start | bytes 12292
  63.3 4.7 slice-start.1
  63.3 4.7 copy-start.14
  91.8 144.2 %all-to-all-start = ((bf16[1024,3,768]{0,1,2:T(4,128)(2,1)}), bf16[1024,3,768]{0,1,2:T(4,128)(2,1)}, u32[]{:S(2)}, u32[]{:S(2)}) async-start(bf16[1024,3,768]{0,1,2:T(4,128)(2,1)} %copy.60), calls=%async_computation | async-start | bytes 12582912 | tf_op jit(solution)/shard_map/all_to_all | solution.py:188
  97.2 235.7 %all-gather.7.cloned.1.call-start = ((), (), s32[]{:S(2)}) async-start(), calls=%async_computation.8 | async-start | bytes 1327104 | tf_op jit(solution)/shard_map/all_gather | solution.py:161
  97.9 273.9 %all-gather.9.cloned.1.call-start = ((), (), s32[]{:S(2)}) async-start(), calls=%async_computation.9 | async-start | bytes 3981312 | tf_op jit(solution)/shard_map/all_gather | solution.py:162
  325.1 41.3 %all-to-all-start.1 = ((bf16[4,1024,192]{1,2,0:T(8,128)(2,1)}), bf16[4,1024,192]{1,2,0:T(8,128)(2,1)}, u32[]{:S(2)}, u32[]{:S(2)}) async-start(bf16[4,1024,192]{1,2,0:T(8,128)(2,1)} %copy.64), calls=%async_computation.1 | async-start | bytes 3145728 | tf_op jit(solution)/shard_map/all_to_all | solution.py:198
  329.5 53.0 %all-gather.11.cloned.1.call-start = ((), (), s32[]{:S(2)}) async-start(), calls=%async_computation.10 | async-start | bytes 1990656 | tf_op jit(solution)/shard_map/all_gather | solution.py:163
  330.1 417.5 %reduce-scatter.7.cloned.1.call-start = ((), (), s32[]{:S(2)}) async-start(), calls=%async_computation.12 | async-start | bytes 2654208 | tf_op jit(solution)/shard_map/reduce_scatter | solution.py:255
  371.8 10.7 %copy-start.16 = (bf16[1024,768]{1,0:T(8,128)(2,1)S(1)}, bf16[1024,768]{1,0:T(8,128)(2,1)}, u32[]{:S(2)}) copy-start(bf16[1024,768]{1,0:T(8,128)(2,1)} %param.19) | copy-start | bytes 4718596
  382.5 14.9 %copy-start.8 = (f32[1024,2304]{1,0:T(8,128)S(1)}, f32[1024,2304]{1,0:T(8,128)}, u32[]{:S(2)}) copy-start(f32[1024,2304]{1,0:T(8,128)} %fusion.91) | copy-start | bytes 28311556
  401.0 9.0 copy-start.10
  417.9 339.9 %reduce-scatter.11.cloned.1.call-start = ((), (), s32[]{:S(2)}) async-start(), calls=%async_computation.14 | async-start | bytes 3981312 | tf_op jit(solution)/shard_map/reduce_scatter | solution.py:257
  428.8 40.0 %all-to-all-start.2 = ((bf16[1024,4,192]{0,2,1:T(8,128)(2,1)}), bf16[1024,4,192]{0,2,1:T(8,128)(2,1)S(1)}, u32[]{:S(2)}, u32[]{:S(2)}) async-start(bf16[1024,4,192]{0,2,1:T(8,128)(2,1)} %bitcast.143), calls=%async_computation.2 | async-start | bytes 3145728 | tf_op jit(solution)/shard_map/all_to_all | solution.py:222
  432.4 327.2 %reduce-scatter.9.cloned.1.call-start = ((), (), s32[]{:S(2)}) async-start(), calls=%async_computation.13 | async-start | bytes 7962624 | tf_op jit(solution)/shard_map/reduce_scatter | solution.py:256
  444.0 380.8 %reduce-scatter.5.cloned.1.call-start = ((), (), s32[]{:S(2)}) async-start(), calls=%async_computation.11 | async-start | bytes 7962624 | tf_op jit(solution)/shard_map/reduce_scatter | solution.py:254
  518.9 4.6 copy-start
  536.3 4.4 copy-start
  633.5 30.9 %collective-permute-start = (bf16[1024,3,192]{0,2,1:T(8,128)(2,1)S(1)}, bf16[1024,3,192]{0,2,1:T(8,128)(2,1)S(1)}, u32[]{:S(2)}, u32[]{:S(2)}) collective-permute-start(bf16[1024,3,192]{0,2,1:T(8,128)(2,1)S(1)} %get-tuple-element.334), channel_id=1, source_target_pairs={{0,1},{1,2},{2,3},{3,0},{4,5},{5,6},{6,7},{7,4},{8,9},{9,10},{10,1... | collective-permute-start | bytes 3538952 | tf_op jit(solution)/shard_map/ppermute | solution.py:34
  633.5 79.6 %collective-permute-start.1 = (bf16[1024,3,192]{0,2,1:T(8,128)(2,1)S(1)}, bf16[1024,3,192]{0,2,1:T(8,128)(2,1)S(1)}, u32[]{:S(2)}, u32[]{:S(2)}) collective-permute-start(bf16[1024,3,192]{0,2,1:T(8,128)(2,1)S(1)} %get-tuple-element.333), channel_id=1, source_target_pairs={{0,2},{1,3},{2,0},{3,1},{4,6},{5,7},{6,4},{7,5},{8,10},{9,11},{10,... | collective-permute-start | bytes 3538952 | tf_op jit(solution)/shard_map/ppermute | solution.py:34
  635.9 77.2 %collective-permute-start.2 = (bf16[1024,3,192]{0,2,1:T(8,128)(2,1)S(1)}, bf16[1024,3,192]{0,2,1:T(8,128)(2,1)S(1)}, u32[]{:S(2)}, u32[]{:S(2)}) collective-permute-start(bf16[1024,3,192]{0,2,1:T(8,128)(2,1)S(1)} %get-tuple-element.332), channel_id=1, source_target_pairs={{0,3},{1,0},{2,1},{3,2},{4,7},{5,4},{6,5},{7,6},{8,11},{9,8},{10,9... | collective-permute-start | bytes 3538952 | tf_op jit(solution)/shard_map/ppermute | solution.py:34
  737.6 150.6 %all-reduce.16.cloned.1.call-start = ((), (), s32[]{:S(2)}) async-start(), calls=%async_computation.15 | async-start | bytes 2506752 | tf_op jit(solution)/shard_map/psum | solution.py:262
  749.2 8.5 copy-start.27
  826.7 30.1 %copy-start.5 = (bf16[1024,768]{0,1:T(8,128)(2,1)S(1)}, bf16[1024,768]{0,1:T(8,128)(2,1)}, u32[]{:S(2)}) copy-start(bf16[1024,768]{0,1:T(8,128)(2,1)} %copy.66) | copy-start | bytes 4718596
  888.2 5.7 copy-start.19
  (23 other events, 63.2 us)
Sparse Core Ops, SparseCore 0:
  9.9 36.7 all-gather.4
  99.9 24.4 all-gather.6
  126.3 33.9 all-gather.8
  331.9 26.9 all-gather.10
  418.0 40.6 reduce-scatter.6
  462.4 48.0 reduce-scatter.10
  514.5 65.4 reduce-scatter.8
  737.7 86.9 reduce-scatter.4
  828.2 59.9 all-reduce.15
